TPU v7x, 32 devices: a whole 2x2x4 slice. The times are simulated.
32 devices in a mesh: dp: 16 (over z, y, core), tensor: 2 (over x).
Axes of the slice: x: 2, y: 2, z: 4, core: 2. Of those that a mesh axis runs over, the one named last changes fastest.
Arguments:
- hidden: bfloat16 [16, 1024, 28672], P('dp', None, 'tensor'), may hold values from -6 to 6
- grad_out: bfloat16 [16, 1024, 8192], P('dp', None, 'tensor'), may hold values from -30 to 30
- proj_in: bfloat16 [64, 28672], P(None, 'tensor'), may hold values from -0.03125 to 0.03125
- proj_out: bfloat16 [64, 8192], P(None, 'tensor'), may hold values from -0.0625 to 0.0625
Outputs:
- covariance: float32 [4096, 4096], P('dp', 'tensor')
All inputs are finite; a program needn't handle non-finite values.
Results may differ from a plain program's by a relative error of at most 0.0003.
Values sent between devices are 32-bit elements; how exact they have to be, the bound alone decides.
A program may use at most 128 MiB of HBM per device.

v0:
```python
import math

import jax
import jax.numpy as jnp
from jax import lax
from jax.sharding import PartitionSpec as P


def outer_sum(panels, width):
    left_side = panels[:, :, :width]
    right_side = panels[:, :, width:]
    return jnp.einsum(
        "sta,stb->sab",
        left_side,
        right_side,
        precision=lax.Precision.HIGHEST,
        preferred_element_type=jnp.float32,
    )


def shards(hidden, grad_out, proj_in, proj_out):
    seqs_here = hidden.shape[0]
    length = hidden.shape[1]
    width = proj_in.shape[0]
    inv_root = 1.0 / math.sqrt(length)
    in_panel = jnp.einsum("stf,af->sta", hidden, proj_in, preferred_element_type=jnp.float32)
    out_panel = jnp.einsum("ste,be->stb", grad_out, proj_out, preferred_element_type=jnp.float32)
    panels = jnp.concatenate([in_panel, out_panel], axis=2)
    summed = lax.psum(panels, "tensor")
    seq_outer = outer_sum(summed, width)
    flat_grads = (seq_outer * inv_root).reshape(seqs_here, width * width)
    total_len = width * width
    col_count = total_len // lax.axis_size("tensor")
    row_count = total_len // lax.axis_size("dp")
    col_begin = lax.axis_index("tensor") * col_count
    row_begin = lax.axis_index("dp") * row_count
    all_seqs = seqs_here * lax.axis_size("dp")
    gathered = lax.all_gather(flat_grads, "dp", axis=0, tiled=True)
    row_part = lax.dynamic_slice_in_dim(gathered, row_begin, row_count, 1)
    col_block = lax.dynamic_slice_in_dim(gathered, col_begin, col_count, 1)
    raw_block = jnp.dot(
        row_part.T, col_block, precision=lax.Precision.HIGHEST, preferred_element_type=jnp.float32
    )
    trace_total = jnp.sum(gathered * gathered)
    damping = 0.5 * trace_total / (all_seqs * total_len)
    row_ids = row_begin + lax.broadcasted_iota(jnp.int32, (row_count, col_count), 0)
    col_ids = col_begin + lax.broadcasted_iota(jnp.int32, (row_count, col_count), 1)
    diagonal = jnp.where(row_ids == col_ids, damping, jnp.float32(0.0))
    return raw_block / all_seqs + diagonal


def solution(mesh):
    placed = (
        P("dp", None, "tensor"),
        P("dp", None, "tensor"),
        P(None, "tensor"),
        P(None, "tensor"),
    )
    return jax.shard_map(
        shards, mesh=mesh, in_specs=placed, out_specs=P("dp", "tensor"), check_vma=False
    )
```

profile of v0, /device:TPU:0, one launch (start us, length us, event | category | flops | bytes accessed | tf_op | source)
XLA Modules:
  0.0 93.0 jit_solution(15729909922945112094)
XLA Ops:
  6.5 0.0 copy-start
  6.5 0.0 copy-start.2
  6.5 0.0 all-reduce.2.cloned.1.call-start
  6.5 1.5 %copy-done = bf16[64,14336]{1,0:T(8,128)(2,1)S(1)} copy-done((bf16[64,14336]{1,0:T(8,128)(2,1)S(1)}, bf16[64,14336]{1,0:T(8,128)(2,1)}, u32[]{:S(2)}) %copy-start) | copy-done | bytes 1835032
  8.0 0.0 copy-start.1
  8.0 14.5 %fusion.8 = f32[1,1024,64]{1,2,0:T(8,128)S(1)} fusion(bf16[64,14336]{1,0:T(8,128)(2,1)S(1)} %copy-done, bf16[1,1024,14336]{2,1,0:T(8,128)(2,1)} %param.4), kind=kOutput, calls=%fused_computation.7 | convolution fusion | flops 1879048192 | bytes 31457280 | tf_op jit(solution)/shard_map/stf,af->sta/dot_general | solution.py:26
  22.5 0.0 copy-done.2
  22.5 0.0 copy-done.1
  22.5 2.7 %fusion.5 = f32[1,1024,64]{1,2,0:T(8,128)S(1)} fusion(bf16[64,4096]{1,0:T(8,128)(2,1)S(1)} %copy-done.2, bf16[1,1024,4096]{2,1,0:T(8,128)(2,1)S(1)} %copy-done.1), kind=kOutput, calls=%fused_computation.6 | convolution fusion | flops 536870912 | bytes 9175040 | tf_op jit(solution)/shard_map/ste,be->stb/dot_general | solution.py:27
  25.2 0.8 pad_maximum_fusion
  26.0 0.0 all-reduce.2.cloned.1.call-update
  26.1 31.4 %all-reduce.2.cloned.1.call-done = f32[1,1024,128]{1,2,0:T(8,128)} async-done(((f32[1,1024,128]{1,2,0:T(8,128)}), f32[1,1024,128]{1,2,0:T(8,128)}) %all-reduce.2.cloned.1.call-update) | async-done | bytes 524304 | tf_op jit(solution)/shard_map/psum | solution.py:29
  57.5 1.4 %convolution_multiply_fusion.1 = f32[64,64]{1,0:T(8,128)S(1)} fusion(f32[1,1024,128]{1,2,0:T(8,128)} %all-reduce.2.cloned.1.call-done), kind=kOutput, calls=%fused_computation.8 | convolution fusion | flops 50335744 | bytes 540672 | tf_op jit(solution)/shard_map/sta,stb->sab/dot_general | solution.py:12
  58.9 0.1 reshape.25
  59.0 22.0 %all-gather = f32[16,1,4096]{2,1,0:T(1,128)S(1)} all-gather(f32[1,1,4096]{2,1,0:T(1,128)S(1)} %reshape.25), channel_id=1, replica_groups=mesh['dp'=16,'tensor'=2] {'dp'}, dimensions={0}, use_global_device_ids=true | all-gather | bytes 278528 | tf_op jit(solution)/shard_map/all_gather | solution.py:38
  81.0 1.1 %multiply_reduce_fusion = f32[]{:T(128)} fusion(f32[16,1,4096]{2,1,0:T(1,128)S(1)} %all-gather), kind=kLoop, calls=%fused_computation.12 | loop fusion | flops 131071 | bytes 262148 | tf_op jit(solution)/shard_map/reduce_sum | solution.py:44
  82.8 3.3 %fusion.4 = f32[256,2048]{1,0:T(8,128)} fusion(f32[]{:T(128)S(6)} %div.11, s32[2048]{0:T(1024)S(1)} %iota_add_fusion, s32[256]{0:T(256)S(1)} %iota_add_fusion.1, f32[16,1,2048]{2,1,0:T(1,128)S(1)} %constant_dynamic-slice_fusion, f32[16,1,256]{2,1,0:T(1,128)S(1)} %constant_dynamic-slice_fusion.1), kind=kOutput, calls=%fused_computation.5 | convolution fusion | flops 102760448 | bytes 2253828 | tf_op jit(solution)/shard_map/dot_general | solution.py:41
  (4 shorter events, 0.0 us)
Async XLA Ops:
  6.5 1.5 %copy-start = (bf16[64,14336]{1,0:T(8,128)(2,1)S(1)}, bf16[64,14336]{1,0:T(8,128)(2,1)}, u32[]{:S(2)}) copy-start(bf16[64,14336]{1,0:T(8,128)(2,1)} %param.6) | copy-start | bytes 5505028
  6.5 16.0 %copy-start.2 = (bf16[64,4096]{1,0:T(8,128)(2,1)S(1)}, bf16[64,4096]{1,0:T(8,128)(2,1)}, u32[]{:S(2)}) copy-start(bf16[64,4096]{1,0:T(8,128)(2,1)} %param.7) | copy-start | bytes 1572868
  6.5 51.0 %all-reduce.2.cloned.1.call-start = ((), (), s32[]{:S(2)}) async-start(), calls=%async_computation | async-start | bytes 1048576 | tf_op jit(solution)/shard_map/psum | solution.py:29
  8.0 14.5 %copy-start.1 = (bf16[1,1024,4096]{2,1,0:T(8,128)(2,1)S(1)}, bf16[1,1024,4096]{2,1,0:T(8,128)(2,1)}, u32[]{:S(2)}) copy-start(bf16[1,1024,4096]{2,1,0:T(8,128)(2,1)} %param.5) | copy-start | bytes 25165828
Sparse Core Ops, SparseCore 0:
  26.2 31.2 all-reduce.1
where the time goes:
time: 93.2 us; the launch traced here: 93 us
  waiting for transfers between devices  31.4 us (34%)
  blocking collectives  22 us (24%)
  matrix products  21.8 us (23%)
  between operations  14.1 us (15%)
  other arithmetic  1.99 us (2%)
  local copies, waits for them, and re-layouts  1.62 us (2%)
    psum x1, waiting for transfers between devices, shards(): summed = lax.psum(panels, 'tensor')  31.4 us
    all_gather x1, blocking collectives, shards(): gathered = lax.all_gather(flat_grads, 'dp', axis=0, tiled=True)  22 us
    dot_general x1, matrix products, shards(): jnp.einsum('stf,af->sta', hidden, proj_in, preferred_element_type=jnp.flo...  14.5 us
    dot_general x1, matrix products, shards(): jnp.dot(row_part.T, col_block, precision=lax.Precision.HIGHEST, preferred...  3.34 us
    dot_general x1, matrix products, shards(): jnp.einsum('ste,be->stb', grad_out, proj_out, preferred_element_type=jnp....  2.66 us
  transfers between devices with their start and end apart: 1, of which 1 were waited for; matrix products, arithmetic and copies ran while one was open for 0% of the time, Pallas kernels for 0%

commit v1 on v0

v1 whole, which is shorter than its diff:
```python
import functools
import math

import jax
import jax.numpy as jnp
from jax import lax
from jax.experimental import pallas as pl
from jax.experimental.pallas import tpu as pltpu
from jax.sharding import PartitionSpec as P

MESH = pl.DeviceIdType.MESH
LANES = 128
AHEAD = 6


def chunk_of(size, largest=1024):
    best = size
    for part in range(LANES, largest + 1, LANES):
        if size % part == 0:
            best = part
    return best


def both_parts(x):
    high = x.astype(jnp.bfloat16)
    low = (x - high.astype(jnp.float32)).astype(jnp.bfloat16)
    return jnp.concatenate([high, low], axis=0)


def contract_last(a, b):
    return lax.dot_general(a, b, (((1,), (1,)), ((), ())), preferred_element_type=jnp.float32)


def grads_kernel(
    n_dp, n_tensor, inv_root,
    hidden, grad_out, proj_in, proj_out,
    cols_out, rows_out, squares_out,
    h_buf, g_buf, wi_buf, wo_buf,
    in_panel, out_panel, out_others, part, flat, mine_in, note, note_in,
    h_sem, g_sem, wi_sem, wo_sem,
    panel_send, panel_recv, part_send, part_recv, cols_send, cols_recv, note_send, note_recv,
):
    dp = lax.axis_index("dp")
    ts = lax.axis_index("tensor")
    h_chunks, _, h_wide = h_buf.shape
    g_chunks, _, g_wide = g_buf.shape
    own_rows = flat.shape[1]
    row_rows = rows_out.shape[1]
    groups = note.shape[0]

    def h_copy(c):
        return pltpu.make_async_copy(
            hidden.at[0, :, pl.ds(pl.multiple_of(c * h_wide, LANES), h_wide)], h_buf.at[c], h_sem.at[c]
        )

    def g_copy(c):
        return pltpu.make_async_copy(
            grad_out.at[0, :, pl.ds(pl.multiple_of(c * g_wide, LANES), g_wide)], g_buf.at[c], g_sem.at[c]
        )

    def wi_copy(c):
        return pltpu.make_async_copy(
            proj_in.at[:, pl.ds(pl.multiple_of(c * h_wide, LANES), h_wide)], wi_buf.at[c], wi_sem.at[c]
        )

    def wo_copy(c):
        return pltpu.make_async_copy(
            proj_out.at[:, pl.ds(pl.multiple_of(c * g_wide, LANES), g_wide)], wo_buf.at[c], wo_sem.at[c]
        )

    copies = [(wo_copy, g_copy, c) for c in range(g_chunks)] + [(wi_copy, h_copy, c) for c in range(h_chunks)]

    def begin(k):
        if k < len(copies):
            weight, data, c = copies[k]
            weight(c).start()
            data(c).start()

    for k in range(AHEAD):
        begin(k)

    barrier = pltpu.get_barrier_semaphore()
    n_all = n_dp * n_tensor

    def greet(i, carry):
        other = lax.rem(dp * n_tensor + ts + i, n_all)
        pl.semaphore_signal(
            barrier, inc=1, device_id=(other // n_tensor, lax.rem(other, n_tensor)), device_id_type=MESH
        )
        return carry

    lax.fori_loop(1, n_all, greet, 0)

    for c in range(g_chunks):
        wo_copy(c).wait()
        g_copy(c).wait()
        begin(c + AHEAD)
        term = contract_last(wo_buf[c], g_buf[c])
        if c == 0:
            out_panel[...] = term
        else:
            out_panel[...] += term

    pl.semaphore_wait(barrier, n_all - 1)

    def panel_copy(i):
        return pltpu.make_async_remote_copy(
            src_ref=out_panel,
            dst_ref=out_others.at[i - 1],
            send_sem=panel_send.at[i - 1],
            recv_sem=panel_recv.at[i - 1],
            device_id=(dp, lax.rem(ts + i, n_tensor)),
            device_id_type=MESH,
        )

    for i in range(1, n_tensor):
        panel_copy(i).start()

    for c in range(h_chunks):
        wi_copy(c).wait()
        h_copy(c).wait()
        begin(g_chunks + c + AHEAD)
        term = contract_last(wi_buf[c], h_buf[c])
        if c == 0:
            in_panel[...] = term
        else:
            in_panel[...] += term

    for i in range(1, n_tensor):
        panel_copy(i).wait()

    total = out_panel[...]
    for i in range(1, n_tensor):
        total = total + out_others[i - 1]
    width = in_panel.shape[0]
    products = contract_last(both_parts(in_panel[...]), both_parts(total))
    sums = products[:width, :width] + products[:width, width:] + products[width:, :width]
    part[...] = sums * inv_root
    even = part[pl.ds(0, width // 2, 2), :]
    odd = part[pl.ds(1, width // 2, 2), :]
    whole = jnp.concatenate([even, odd], axis=1)
    for j in range(n_tensor):
        flat[j] = whole[j * own_rows:(j + 1) * own_rows]

    def part_copy(i):
        to = lax.rem(ts + i, n_tensor)
        return pltpu.make_async_remote_copy(
            src_ref=flat.at[to],
            dst_ref=mine_in.at[i - 1],
            send_sem=part_send.at[i - 1],
            recv_sem=part_recv.at[i - 1],
            device_id=(dp, to),
            device_id_type=MESH,
        )

    for i in range(1, n_tensor):
        part_copy(i).start()
    for i in range(1, n_tensor):
        part_copy(i).wait()
    mine = flat[ts]
    for i in range(1, n_tensor):
        mine = mine + mine_in[i - 1]
    cols_out[0] = mine
    square = jnp.sum(mine * mine)
    for k in range(groups):
        note[k, :row_rows] = mine[k * row_rows:(k + 1) * row_rows]
        note[k, row_rows:] = jnp.full((note.shape[1] - row_rows, LANES), square, jnp.float32)

    def cols_copy(i):
        return pltpu.make_async_remote_copy(
            src_ref=cols_out.at[0],
            dst_ref=cols_out.at[i],
            send_sem=cols_send.at[i],
            recv_sem=cols_recv.at[i],
            device_id=(lax.rem(dp + i, n_dp), ts),
            device_id_type=MESH,
        )

    def note_copy(j, i):
        to = lax.rem(dp + i, n_dp)
        return pltpu.make_async_remote_copy(
            src_ref=note.at[lax.rem(to, groups)],
            dst_ref=note_in.at[j - 1, i],
            send_sem=note_send.at[j - 1, i],
            recv_sem=note_recv.at[j - 1, i],
            device_id=(to, lax.rem(ts + j, n_tensor)),
            device_id_type=MESH,
        )

    def start_cols(i, carry):
        cols_copy(i).start()
        return carry

    def wait_cols(i, carry):
        cols_copy(i).wait()
        return carry

    lax.fori_loop(1, n_dp, start_cols, 0)
    for j in range(1, n_tensor):
        def start_notes(i, carry):
            note_copy(j, i).start()
            return carry

        lax.fori_loop(0, n_dp, start_notes, 0)
    lax.fori_loop(1, n_dp, wait_cols, 0)
    for j in range(1, n_tensor):
        def wait_notes(i, carry):
            note_copy(j, i).wait()
            return carry

        lax.fori_loop(0, n_dp, wait_notes, 0)

    owner = dp // groups
    first = lax.rem(dp, groups)
    for k in range(groups):
        @pl.when(jnp.logical_and(owner == ts, first == k))
        def _():
            rows_out[...] = cols_out[:, k * row_rows:(k + 1) * row_rows]

    squares = jnp.sum(cols_out[...] * cols_out[...])
    for j in range(1, n_tensor):
        @pl.when(owner == lax.rem(ts + n_tensor - j, n_tensor))
        def _():
            rows_out[...] = note_in[j - 1, :, :row_rows]

    others = jnp.zeros((1, LANES), jnp.float32)
    for j in range(1, n_tensor):
        others = others + jnp.sum(note_in[j - 1, :, row_rows], axis=0, keepdims=True)
    squares_out[...] = jnp.broadcast_to(others + squares, squares_out.shape)


def covariance_kernel(n_dp, n_tensor, seqs, total_len, cols, rows, squares, out):
    dp = lax.axis_index("dp")
    ts = lax.axis_index("tensor")
    height, wide = out.shape
    step = pl.program_id(0)
    row_rows = height // LANES
    col_rows = cols.shape[0] // seqs
    here = wide // LANES
    row_tiles = [rows[pl.ds(k, seqs, row_rows), :] for k in range(row_rows)]
    col_tiles = [cols[pl.ds(step * here + k, seqs, col_rows), :] for k in range(here)]
    left = jnp.concatenate(row_tiles, axis=1) * (1.0 / seqs)
    right = jnp.concatenate(col_tiles, axis=1)
    left_hi = left.astype(jnp.bfloat16).astype(jnp.float32)
    left_lo = left - left_hi
    right_hi = right.astype(jnp.bfloat16).astype(jnp.float32)
    right_lo = right - right_hi
    a = jnp.concatenate([left_hi, left_lo, left_hi], axis=0).T.astype(jnp.bfloat16)
    b = jnp.concatenate([right_hi, right_hi, right_lo], axis=0).astype(jnp.bfloat16)
    raw = jnp.dot(a, b, preferred_element_type=jnp.float32)
    damping = squares[0, 0] * (0.5 / (seqs * total_len))
    row_ids = dp * height + lax.broadcasted_iota(jnp.int32, out.shape, 0)
    col_begin = ts * (cols.shape[0] // seqs * LANES) + step * wide
    col_ids = col_begin + lax.broadcasted_iota(jnp.int32, out.shape, 1)
    out[...] = raw + jnp.where(row_ids == col_ids, damping, jnp.float32(0.0))


def shards(n_dp, n_tensor, hidden, grad_out, proj_in, proj_out):
    seqs_here, length, units = hidden.shape
    assert seqs_here == 1
    feats = grad_out.shape[2]
    width = proj_in.shape[0]
    total_len = width * width
    flat_rows = total_len // LANES
    own_rows = flat_rows // n_tensor
    row_rows = flat_rows // n_dp
    groups = own_rows // row_rows
    assert groups * row_rows == own_rows and groups * n_tensor == n_dp
    h_wide, g_wide = chunk_of(units), chunk_of(feats)
    h_chunks, g_chunks = units // h_wide, feats // g_wide
    peers = max(n_tensor - 1, 1)
    note_rows = row_rows + 1
    f32, bf16 = jnp.float32, jnp.bfloat16
    vmem = pl.BlockSpec(memory_space=pltpu.VMEM)
    anywhere = pl.BlockSpec(memory_space=pl.ANY)
    dma = pltpu.SemaphoreType.DMA
    cols, rows, squares = pl.pallas_call(
        functools.partial(grads_kernel, n_dp, n_tensor, 1.0 / math.sqrt(length)),
        out_shape=(
            jax.ShapeDtypeStruct((n_dp, own_rows, LANES), f32),
            jax.ShapeDtypeStruct((n_dp, row_rows, LANES), f32),
            jax.ShapeDtypeStruct((8, LANES), f32),
        ),
        in_specs=[anywhere] * 4,
        out_specs=(vmem, vmem, vmem),
        scratch_shapes=[
            pltpu.VMEM((h_chunks, length, h_wide), bf16),
            pltpu.VMEM((g_chunks, length, g_wide), bf16),
            pltpu.VMEM((h_chunks, width, h_wide), bf16),
            pltpu.VMEM((g_chunks, width, g_wide), bf16),
            pltpu.VMEM((width, length), f32),
            pltpu.VMEM((width, length), f32),
            pltpu.VMEM((peers, width, length), f32),
            pltpu.VMEM((width, width), f32),
            pltpu.VMEM((n_tensor, own_rows, LANES), f32),
            pltpu.VMEM((peers, own_rows, LANES), f32),
            pltpu.VMEM((groups, note_rows, LANES), f32),
            pltpu.VMEM((peers, n_dp, note_rows, LANES), f32),
            dma((h_chunks,)),
            dma((g_chunks,)),
            dma((h_chunks,)),
            dma((g_chunks,)),
            dma((peers,)),
            dma((peers,)),
            dma((peers,)),
            dma((peers,)),
            dma((n_dp,)),
            dma((n_dp,)),
            dma((peers, n_dp)),
            dma((peers, n_dp)),
        ],
        compiler_params=pltpu.CompilerParams(
            collective_id=0, has_side_effects=True, vmem_limit_bytes=56 * 1024 * 1024
        ),
        cost_estimate=pl.CostEstimate(
            flops=2 * length * width * (units + feats),
            bytes_accessed=2 * (length + width) * (units + feats),
            transcendentals=0,
        ),
        name="projected_grads",
    )(hidden, grad_out, proj_in, proj_out)
    height, wide = total_len // n_dp, total_len // n_tensor
    block = min(wide, 512)
    return pl.pallas_call(
        functools.partial(covariance_kernel, n_dp, n_tensor, n_dp, total_len),
        out_shape=jax.ShapeDtypeStruct((height, wide), f32),
        grid=(wide // block,),
        in_specs=[vmem] * 3,
        out_specs=pl.BlockSpec((height, block), lambda i: (0, i)),
        name="covariance",
    )(
        cols.reshape(n_dp * own_rows, LANES),
        rows.reshape(n_dp * row_rows, LANES),
        squares,
    )


def solution(mesh):
    placed = (
        P("dp", None, "tensor"),
        P("dp", None, "tensor"),
        P(None, "tensor"),
        P(None, "tensor"),
    )
    return jax.shard_map(
        functools.partial(shards, mesh.shape["dp"], mesh.shape["tensor"]),
        mesh=mesh, in_specs=placed, out_specs=P("dp", "tensor"), check_vma=False,
    )
```

time: 93.2 us -> 31.9 us (0.34)
  Pallas kernels: 0 us -> 31.8 us
  waiting for transfers between devices: 31.4 us -> 0 us
  blocking collectives: 22 us -> 0 us
  matrix products: 21.8 us -> 0 us
  between operations: 14.1 us -> 0.01 us
  other arithmetic: 1.99 us -> 0 us
  local copies, waits for them, and re-layouts: 1.62 us -> 0 us
    pallas_call x0 -> x2, Pallas kernels: none -> 31.8 us  [the longest x1 28.4 us: shards(): pl.pallas_call(functools.partial(grads_kernel, n_dp, n_tensor, 1.0 / math...]
    psum x1 -> x0, waiting for transfers between devices: 31.4 us -> none  [shards(): summed = lax.psum(panels, 'tensor')]
    all_gather x1 -> x0, blocking collectives: 22 us -> none  [shards(): gathered = lax.all_gather(flat_grads, 'dp', axis=0, tiled=True)]
    dot_general x4 -> x0, matrix products: 21.8 us -> none  [the longest x1 14.5 us: shards(): jnp.einsum('stf,af->sta', hidden, proj_in, preferred_element_type=jnp.flo...]
    unnamed x7 -> x0, local copies, waits for them, and re-layouts: 1.59 us -> none
    reduce_sum x1 -> x0, other arithmetic: 1.14 us -> none  [shards(): trace_total = jnp.sum(gathered * gathered)]
  transfers between devices with their start and end apart: 1 -> 0, of which waited for: 1 -> 0; matrix products, arithmetic and copies ran while one was open for 0% -> 0% of each run, Pallas kernels for 0% -> 0%
where the time goes in v1:
time: 31.9 us; the launch traced here: 31.8 us
  Pallas kernels  31.8 us (100%)
    pallas_call x1, Pallas kernels, shards(): pl.pallas_call(functools.partial(grads_kernel, n_dp, n_tensor, 1.0 / math...  28.4 us
    pallas_call x1, Pallas kernels, shards(): pl.pallas_call(functools.partial(covariance_kernel, n_dp, n_tensor, n_dp,...  3.36 us

profile of v1, /device:TPU:0, one launch (start us, length us, event | category | flops | bytes accessed | tf_op | source)
XLA Modules:
  0.0 31.8 jit_solution(15216514529146350137)
XLA Ops:
  0.0 28.4 %projected_grads.1 = (f32[16,16,128]{2,1,0:T(8,128)}, f32[16,2,128]{2,1,0:T(2,128)}, f32[8,128]{1,0:T(8,128)}) custom-call(bf16[1,1024,14336]{2,1,0:T(8,128)(2,1)} %hidden.1, bf16[1,1024,4096]{2,1,0:T(8,128)(2,1)} %grad_out.1, bf16[64,14336]{1,0:T(8,128)(2,1)} %proj_in.1, bf16[64,4096]{1,0:T(8,128)(2,1)} %proj_out.1), custom_call_target="tpu_custom_call" | custom-call | flops 2415919104 | bytes 40108032 | tf_op jit(solution)/shard_map/projected_grads/pallas_call | solution.py:277
  28.4 3.4 %covariance.1 = f32[256,2048]{1,0:T(8,128)} custom-call(f32[256,128]{1,0:T(8,128)} %bitcast.2, f32[32,128]{1,0:T(8,128)} %bitcast.3, f32[8,128]{1,0:T(8,128)} %get-tuple-element.10.squares), custom_call_target="tpu_custom_call" | custom-call | tf_op jit(solution)/shard_map/covariance/pallas_call | solution.py:324

commit v2 on v1

--- a/solution.py
+++ b/solution.py
@@ -35,7 +35,7 @@
     n_dp, n_tensor, inv_root,
     hidden, grad_out, proj_in, proj_out,
     cols_out, rows_out, squares_out,
-    h_buf, g_buf, wi_buf, wo_buf,
+    h_buf, g_buf, wi_buf, wo_buf, tokens,
     in_panel, out_panel, out_others, part, flat, mine_in, note, note_in,
     h_sem, g_sem, wi_sem, wo_sem,
     panel_send, panel_recv, part_send, part_recv, cols_send, cols_recv, note_send, note_recv,
@@ -95,11 +95,12 @@
         wo_copy(c).wait()
         g_copy(c).wait()
         begin(c + AHEAD)
-        term = contract_last(wo_buf[c], g_buf[c])
+        term = contract_last(g_buf[c], wo_buf[c])
         if c == 0:
-            out_panel[...] = term
+            tokens[...] = term
         else:
-            out_panel[...] += term
+            tokens[...] += term
+    out_panel[...] = tokens[...].T
 
     pl.semaphore_wait(barrier, n_all - 1)
 
@@ -120,11 +121,12 @@
         wi_copy(c).wait()
         h_copy(c).wait()
         begin(g_chunks + c + AHEAD)
-        term = contract_last(wi_buf[c], h_buf[c])
+        term = contract_last(h_buf[c], wi_buf[c])
         if c == 0:
-            in_panel[...] = term
+            tokens[...] = term
         else:
-            in_panel[...] += term
+            tokens[...] += term
+    in_panel[...] = tokens[...].T
 
     for i in range(1, n_tensor):
         panel_copy(i).wait()
@@ -288,6 +290,7 @@
             pltpu.VMEM((g_chunks, length, g_wide), bf16),
             pltpu.VMEM((h_chunks, width, h_wide), bf16),
             pltpu.VMEM((g_chunks, width, g_wide), bf16),
+            pltpu.VMEM((length, width), f32),
             pltpu.VMEM((width, length), f32),
             pltpu.VMEM((width, length), f32),
             pltpu.VMEM((peers, width, length), f32),

time: 31.9 us -> 34.2 us (1.072)
  Pallas kernels: 31.8 us -> 34.1 us
    pallas_call x1, Pallas kernels: 28.4 us -> 30.7 us  [shards(): pl.pallas_call(functools.partial(grads_kernel, n_dp, n_tensor, 1.0 / math...]
where the time goes in v2:
time: 34.2 us; the launch traced here: 34.1 us
  Pallas kernels  34.1 us (100%)
    pallas_call x1, Pallas kernels, shards(): pl.pallas_call(functools.partial(grads_kernel, n_dp, n_tensor, 1.0 / math...  30.7 us
    pallas_call x1, Pallas kernels, shards(): pl.pallas_call(functools.partial(covariance_kernel, n_dp, n_tensor, n_dp,...  3.37 us

profile of v2, /device:TPU:0, one launch (start us, length us, event | category | flops | bytes accessed | tf_op | source)
XLA Modules:
  0.0 34.1 jit_solution(17614355740084303538)
XLA Ops:
  0.0 30.7 %projected_grads.1 = (f32[16,16,128]{2,1,0:T(8,128)}, f32[16,2,128]{2,1,0:T(2,128)}, f32[8,128]{1,0:T(8,128)}) custom-call(bf16[1,1024,14336]{2,1,0:T(8,128)(2,1)} %hidden.1, bf16[1,1024,4096]{2,1,0:T(8,128)(2,1)} %grad_out.1, bf16[64,14336]{1,0:T(8,128)(2,1)} %proj_in.1, bf16[64,4096]{1,0:T(8,128)(2,1)} %proj_out.1), custom_call_target="tpu_custom_call" | custom-call | flops 2415919104 | bytes 40108032 | tf_op jit(solution)/shard_map/projected_grads/pallas_call | solution.py:279
  30.7 3.4 %covariance.1 = f32[256,2048]{1,0:T(8,128)} custom-call(f32[256,128]{1,0:T(8,128)} %bitcast.2, f32[32,128]{1,0:T(8,128)} %bitcast.3, f32[8,128]{1,0:T(8,128)} %get-tuple-element.10.squares), custom_call_target="tpu_custom_call" | custom-call | tf_op jit(solution)/shard_map/covariance/pallas_call | solution.py:327

commit v3 on v1

v3 whole, which is shorter than its diff:
```python
import functools
import math

import jax
import jax.numpy as jnp
from jax import lax
from jax.experimental import pallas as pl
from jax.experimental.pallas import tpu as pltpu
from jax.sharding import PartitionSpec as P

MESH = pl.DeviceIdType.MESH
LANES = 128
AHEAD = 6


def chunk_of(size, largest=1024):
    best = size
    for part in range(LANES, largest + 1, LANES):
        if size % part == 0:
            best = part
    return best


def both_parts(x):
    high = x.astype(jnp.bfloat16)
    low = (x - high.astype(jnp.float32)).astype(jnp.bfloat16)
    return jnp.concatenate([high, low], axis=0)


def contract_last(a, b):
    return lax.dot_general(a, b, (((1,), (1,)), ((), ())), preferred_element_type=jnp.float32)


def grads_kernel(
    n_dp, n_tensor, inv_root,
    hidden, grad_out, proj_in, proj_out,
    gathered,
    h_buf, g_buf, wi_buf, wo_buf,
    in_panel, out_panel, out_others, part, flat, flat_others, message,
    h_sem, g_sem, wi_sem, wo_sem,
    panel_send, panel_recv, part_send, part_recv, message_send, message_recv,
):
    dp = lax.axis_index("dp")
    ts = lax.axis_index("tensor")
    h_chunks, _, h_wide = h_buf.shape
    g_chunks, _, g_wide = g_buf.shape
    flat_rows = flat.shape[0]
    own_rows = flat_rows // n_tensor
    row_rows = flat_rows // n_dp
    used = own_rows + row_rows + 1

    def h_copy(c):
        return pltpu.make_async_copy(
            hidden.at[0, :, pl.ds(pl.multiple_of(c * h_wide, LANES), h_wide)], h_buf.at[c], h_sem.at[c]
        )

    def g_copy(c):
        return pltpu.make_async_copy(
            grad_out.at[0, :, pl.ds(pl.multiple_of(c * g_wide, LANES), g_wide)], g_buf.at[c], g_sem.at[c]
        )

    def wi_copy(c):
        return pltpu.make_async_copy(
            proj_in.at[:, pl.ds(pl.multiple_of(c * h_wide, LANES), h_wide)], wi_buf.at[c], wi_sem.at[c]
        )

    def wo_copy(c):
        return pltpu.make_async_copy(
            proj_out.at[:, pl.ds(pl.multiple_of(c * g_wide, LANES), g_wide)], wo_buf.at[c], wo_sem.at[c]
        )

    copies = [(wo_copy, g_copy, c) for c in range(g_chunks)] + [(wi_copy, h_copy, c) for c in range(h_chunks)]

    def begin(k):
        if k < len(copies):
            weight, data, c = copies[k]
            weight(c).start()
            data(c).start()

    for k in range(AHEAD):
        begin(k)

    barrier = pltpu.get_barrier_semaphore()
    n_all = n_dp * n_tensor

    def greet(i, carry):
        other = lax.rem(dp * n_tensor + ts + i, n_all)
        pl.semaphore_signal(
            barrier, inc=1, device_id=(other // n_tensor, lax.rem(other, n_tensor)), device_id_type=MESH
        )
        return carry

    lax.fori_loop(1, n_all, greet, 0)

    for c in range(g_chunks):
        wo_copy(c).wait()
        g_copy(c).wait()
        begin(c + AHEAD)
        term = contract_last(wo_buf[c], g_buf[c])
        if c == 0:
            out_panel[...] = term
        else:
            out_panel[...] += term

    pl.semaphore_wait(barrier, n_all - 1)

    def panel_copy(i):
        return pltpu.make_async_remote_copy(
            src_ref=out_panel,
            dst_ref=out_others.at[i - 1],
            send_sem=panel_send.at[i - 1],
            recv_sem=panel_recv.at[i - 1],
            device_id=(dp, lax.rem(ts + i, n_tensor)),
            device_id_type=MESH,
        )

    for i in range(1, n_tensor):
        panel_copy(i).start()

    for c in range(h_chunks):
        wi_copy(c).wait()
        h_copy(c).wait()
        begin(g_chunks + c + AHEAD)
        term = contract_last(wi_buf[c], h_buf[c])
        if c == 0:
            in_panel[...] = term
        else:
            in_panel[...] += term

    for i in range(1, n_tensor):
        panel_copy(i).wait()

    total = out_panel[...]
    for i in range(1, n_tensor):
        total = total + out_others[i - 1]
    width = in_panel.shape[0]
    products = contract_last(both_parts(in_panel[...]), both_parts(total))
    sums = products[:width, :width] + products[:width, width:] + products[width:, :width]
    part[...] = sums * inv_root
    even = part[pl.ds(0, width // 2, 2), :]
    odd = part[pl.ds(1, width // 2, 2), :]
    flat[...] = jnp.concatenate([even, odd], axis=1)

    def part_copy(i):
        return pltpu.make_async_remote_copy(
            src_ref=flat,
            dst_ref=flat_others.at[i - 1],
            send_sem=part_send.at[i - 1],
            recv_sem=part_recv.at[i - 1],
            device_id=(dp, lax.rem(ts + i, n_tensor)),
            device_id_type=MESH,
        )

    for i in range(1, n_tensor):
        part_copy(i).start()
    for i in range(1, n_tensor):
        part_copy(i).wait()
    grads = flat[...]
    for i in range(1, n_tensor):
        grads = grads + flat_others[i - 1]
    mine = grads[:own_rows]
    for j in range(1, n_tensor):
        mine = jnp.where(ts == j, grads[j * own_rows:(j + 1) * own_rows], mine)
    square = jnp.broadcast_to(jnp.sum(grads * grads), (1, LANES))
    for d in range(n_dp):
        message[d, :own_rows] = mine
        message[d, own_rows:own_rows + row_rows] = grads[d * row_rows:(d + 1) * row_rows]
        message[d, own_rows + row_rows:used] = square

    def message_copy(i):
        to = lax.rem(dp + i, n_dp)
        return pltpu.make_async_remote_copy(
            src_ref=message.at[to, pl.ds(0, used)],
            dst_ref=gathered.at[i, pl.ds(0, used)],
            send_sem=message_send.at[i],
            recv_sem=message_recv.at[i],
            device_id=(to, ts),
            device_id_type=MESH,
        )

    for i in range(1, n_dp):
        message_copy(i).start()
    gathered[0] = message[dp]
    for i in range(1, n_dp):
        message_copy(i).wait()


def covariance_kernel(n_dp, n_tensor, total_len, gathered, out, block_sem, result):
    dp = lax.axis_index("dp")
    ts = lax.axis_index("tensor")
    height, wide = out.shape
    row_rows = height // LANES
    own_rows = wide // LANES
    slot = gathered.shape[0] // n_dp
    blocks, _, block = result.shape
    here = block // LANES

    def high_low(first, count):
        tiles = [gathered[pl.ds(first + k, n_dp, slot), :] for k in range(count)]
        x = jnp.concatenate(tiles, axis=1)
        high = x.astype(jnp.bfloat16).astype(jnp.float32)
        return high, x - high

    left_high, left_low = high_low(own_rows, row_rows)
    left = jnp.concatenate([left_high, left_low, left_high], axis=0) * (1.0 / n_dp)
    left = left.T.astype(jnp.bfloat16)
    squares = jnp.sum(gathered[pl.ds(own_rows + row_rows, n_dp, slot), :], axis=0, keepdims=True)
    damping = squares * (0.5 / (n_dp * total_len))
    diagonal = dp * height - ts * wide

    def block_copy(b):
        return pltpu.make_async_copy(result.at[b], out.at[:, pl.ds(b * block, block)], block_sem.at[b])

    for b in range(blocks):
        right_high, right_low = high_low(b * here, here)
        right = jnp.concatenate([right_high, right_high, right_low], axis=0).astype(jnp.bfloat16)
        result[b] = jnp.dot(left, right, preferred_element_type=jnp.float32)
        for k in range(block // height):
            @pl.when(diagonal == b * block + k * height)
            def _():
                for r in range(row_rows):
                    place = (pl.ds(r * LANES, LANES), pl.ds(k * height + r * LANES, LANES))
                    ids = lax.broadcasted_iota(jnp.int32, (LANES, LANES), 0)
                    same = ids == lax.broadcasted_iota(jnp.int32, (LANES, LANES), 1)
                    result[(b, *place)] += jnp.where(same, damping, jnp.float32(0.0))
        block_copy(b).start()
    for b in range(blocks):
        block_copy(b).wait()


def shards(n_dp, n_tensor, hidden, grad_out, proj_in, proj_out):
    seqs_here, length, units = hidden.shape
    assert seqs_here == 1
    feats = grad_out.shape[2]
    width = proj_in.shape[0]
    total_len = width * width
    flat_rows = total_len // LANES
    own_rows = flat_rows // n_tensor
    row_rows = flat_rows // n_dp
    slot = -(-(own_rows + row_rows + 1) // 8) * 8
    h_wide, g_wide = chunk_of(units), chunk_of(feats)
    h_chunks, g_chunks = units // h_wide, feats // g_wide
    peers = max(n_tensor - 1, 1)
    f32, bf16 = jnp.float32, jnp.bfloat16
    vmem = pl.BlockSpec(memory_space=pltpu.VMEM)
    in_hbm = pl.BlockSpec(memory_space=pltpu.HBM)
    dma = pltpu.SemaphoreType.DMA
    gathered = pl.pallas_call(
        functools.partial(grads_kernel, n_dp, n_tensor, 1.0 / math.sqrt(length)),
        out_shape=jax.ShapeDtypeStruct((n_dp, slot, LANES), f32),
        in_specs=[in_hbm] * 4,
        out_specs=vmem,
        scratch_shapes=[
            pltpu.VMEM((h_chunks, length, h_wide), bf16),
            pltpu.VMEM((g_chunks, length, g_wide), bf16),
            pltpu.VMEM((h_chunks, width, h_wide), bf16),
            pltpu.VMEM((g_chunks, width, g_wide), bf16),
            pltpu.VMEM((width, length), f32),
            pltpu.VMEM((width, length), f32),
            pltpu.VMEM((peers, width, length), f32),
            pltpu.VMEM((width, width), f32),
            pltpu.VMEM((flat_rows, LANES), f32),
            pltpu.VMEM((peers, flat_rows, LANES), f32),
            pltpu.VMEM((n_dp, slot, LANES), f32),
            dma((h_chunks,)),
            dma((g_chunks,)),
            dma((h_chunks,)),
            dma((g_chunks,)),
            dma((peers,)),
            dma((peers,)),
            dma((peers,)),
            dma((peers,)),
            dma((n_dp,)),
            dma((n_dp,)),
        ],
        compiler_params=pltpu.CompilerParams(
            collective_id=0, has_side_effects=True, vmem_limit_bytes=50 * 1024 * 1024
        ),
        cost_estimate=pl.CostEstimate(
            flops=2 * length * width * (units + feats),
            bytes_accessed=2 * (length + width) * (units + feats),
            transcendentals=0,
        ),
        name="projected_grads",
    )(*(pltpu.with_memory_space_constraint(x, pltpu.HBM) for x in (hidden, grad_out, proj_in, proj_out)))
    height, wide = total_len // n_dp, total_len // n_tensor
    block = min(wide, 512)
    return pl.pallas_call(
        functools.partial(covariance_kernel, n_dp, n_tensor, total_len),
        out_shape=jax.ShapeDtypeStruct((height, wide), f32),
        in_specs=[vmem],
        out_specs=pl.BlockSpec(memory_space=pltpu.HBM),
        scratch_shapes=[dma((wide // block,)), pltpu.VMEM((wide // block, height, block), f32)],
        compiler_params=pltpu.CompilerParams(vmem_limit_bytes=16 * 1024 * 1024),
        name="covariance",
    )(gathered.reshape(n_dp * slot, LANES))


def solution(mesh):
    placed = (
        P("dp", None, "tensor"),
        P("dp", None, "tensor"),
        P(None, "tensor"),
        P(None, "tensor"),
    )
    return jax.shard_map(
        functools.partial(shards, mesh.shape["dp"], mesh.shape["tensor"]),
        mesh=mesh, in_specs=placed, out_specs=P("dp", "tensor"), check_vma=False,
    )
```

time: 31.9 us -> 28.2 us (0.88)
  Pallas kernels: 31.8 us -> 28.1 us
    pallas_call x1, Pallas kernels: 28.4 us -> 26.4 us  [shards(): pl.pallas_call(functools.partial(grads_kernel, n_dp, n_tensor, 1.0 / math...]
    pallas_call x1, Pallas kernels: 3.36 us -> 1.72 us  [shards(): pl.pallas_call(functools.partial(covariance_kernel, n_dp, n_tensor, total...]
where the time goes in v3:
time: 28.2 us; the launch traced here: 28.1 us
  Pallas kernels  28.1 us (100%)
    pallas_call x1, Pallas kernels, shards(): pl.pallas_call(functools.partial(grads_kernel, n_dp, n_tensor, 1.0 / math...  26.4 us
    pallas_call x1, Pallas kernels, shards(): pl.pallas_call(functools.partial(covariance_kernel, n_dp, n_tensor, total...  1.72 us

profile of v3, /device:TPU:0, one launch (start us, length us, event | category | flops | bytes accessed | tf_op | source)
XLA Modules:
  0.0 28.1 jit_solution(14777399226502587533)
XLA Ops:
  0.0 26.4 %projected_grads.1 = f32[16,24,128]{2,1,0:T(8,128)S(1)} custom-call(bf16[1,1024,14336]{2,1,0:T(8,128)(2,1)} %hidden.1, bf16[1,1024,4096]{2,1,0:T(8,128)(2,1)} %grad_out.1, bf16[64,14336]{1,0:T(8,128)(2,1)} %proj_in.1, bf16[64,4096]{1,0:T(8,128)(2,1)} %proj_out.1), custom_call_target="tpu_custom_call" | custom-call | flops 2415919104 | bytes 40108032 | tf_op jit(solution)/shard_map/projected_grads/pallas_call | solution.py:248
  26.4 1.7 %covariance.1 = f32[256,2048]{1,0:T(8,128)} custom-call(f32[384,128]{1,0:T(8,128)S(1)} %bitcast.1), custom_call_target="tpu_custom_call" | custom-call | tf_op jit(solution)/shard_map/covariance/pallas_call | solution.py:288

commit v4 on v3

--- a/solution.py
+++ b/solution.py
@@ -21,6 +21,15 @@
     return best
 
 
+def groups_of(count, first, last):
+    runs, c = [], 0
+    while c < count:
+        size = 1 if c < first or c >= count - last or c + 1 >= count - last else 2
+        runs.append(list(range(c, c + size)))
+        c += size
+    return runs
+
+
 def both_parts(x):
     high = x.astype(jnp.bfloat16)
     low = (x - high.astype(jnp.float32)).astype(jnp.bfloat16)
@@ -36,7 +45,7 @@
     hidden, grad_out, proj_in, proj_out,
     gathered,
     h_buf, g_buf, wi_buf, wo_buf,
-    in_panel, out_panel, out_others, part, flat, flat_others, message,
+    in_panel, out_panel, out_others, total_parts, part, flat, flat_others, message,
     h_sem, g_sem, wi_sem, wo_sem,
     panel_send, panel_recv, part_send, part_recv, message_send, message_recv,
 ):
@@ -92,15 +101,21 @@
 
     lax.fori_loop(1, n_all, greet, 0)
 
-    for c in range(g_chunks):
-        wo_copy(c).wait()
-        g_copy(c).wait()
-        begin(c + AHEAD)
-        term = contract_last(wo_buf[c], g_buf[c])
-        if c == 0:
-            out_panel[...] = term
+    def project(group, weights, data, weight_copy, data_copy, before, panel):
+        for c in group:
+            weight_copy(c).wait()
+            data_copy(c).wait()
+            begin(before + c + AHEAD)
+        term = contract_last(weights[group[0]], data[group[0]])
+        for c in group[1:]:
+            term = term + contract_last(weights[c], data[c])
+        if group[0] == 0:
+            panel[...] = term
         else:
-            out_panel[...] += term
+            panel[...] += term
+
+    for group in groups_of(g_chunks, 1, 0):
+        project(group, wo_buf, g_buf, wo_copy, g_copy, 0, out_panel)
 
     pl.semaphore_wait(barrier, n_all - 1)
 
@@ -117,24 +132,19 @@
     for i in range(1, n_tensor):
         panel_copy(i).start()
 
-    for c in range(h_chunks):
-        wi_copy(c).wait()
-        h_copy(c).wait()
-        begin(g_chunks + c + AHEAD)
-        term = contract_last(wi_buf[c], h_buf[c])
-        if c == 0:
-            in_panel[...] = term
-        else:
-            in_panel[...] += term
-
+    in_groups = groups_of(h_chunks, 0, 2)
+    for group in in_groups[:-1]:
+        project(group, wi_buf, h_buf, wi_copy, h_copy, g_chunks, in_panel)
     for i in range(1, n_tensor):
         panel_copy(i).wait()
-
     total = out_panel[...]
     for i in range(1, n_tensor):
         total = total + out_others[i - 1]
+    total_parts[...] = both_parts(total)
+    project(in_groups[-1], wi_buf, h_buf, wi_copy, h_copy, g_chunks, in_panel)
+
     width = in_panel.shape[0]
-    products = contract_last(both_parts(in_panel[...]), both_parts(total))
+    products = contract_last(both_parts(in_panel[...]), total_parts[...])
     sums = products[:width, :width] + products[:width, width:] + products[width:, :width]
     part[...] = sums * inv_root
     even = part[pl.ds(0, width // 2, 2), :]
@@ -178,7 +188,7 @@
             device_id_type=MESH,
         )
 
-    for i in range(1, n_dp):
+    for i in sorted(range(1, n_dp), key=lambda i: -min(i, n_dp - i)):
         message_copy(i).start()
     gathered[0] = message[dp]
     for i in range(1, n_dp):
@@ -258,6 +268,7 @@
             pltpu.VMEM((width, length), f32),
             pltpu.VMEM((width, length), f32),
             pltpu.VMEM((peers, width, length), f32),
+            pltpu.VMEM((2 * width, length), bf16),
             pltpu.VMEM((width, width), f32),
             pltpu.VMEM((flat_rows, LANES), f32),
             pltpu.VMEM((peers, flat_rows, LANES), f32),

time: 28.2 us -> 29.3 us (1.039)
  Pallas kernels: 28.1 us -> 29.2 us
    pallas_call x1, Pallas kernels: 26.4 us -> 27.4 us  [shards(): pl.pallas_call(functools.partial(grads_kernel, n_dp, n_tensor, 1.0 / math...]
where the time goes in v4:
time: 29.3 us; the launch traced here: 29.2 us
  Pallas kernels  29.2 us (100%)
    pallas_call x1, Pallas kernels, shards(): pl.pallas_call(functools.partial(grads_kernel, n_dp, n_tensor, 1.0 / math...  27.4 us
    pallas_call x1, Pallas kernels, shards(): pl.pallas_call(functools.partial(covariance_kernel, n_dp, n_tensor, total...  1.72 us

profile of v4, /device:TPU:0, one launch (start us, length us, event | category | flops | bytes accessed | tf_op | source)
XLA Modules:
  0.0 29.2 jit_solution(13689045018345360356)
XLA Ops:
  0.0 27.4 %projected_grads.1 = f32[16,24,128]{2,1,0:T(8,128)S(1)} custom-call(bf16[1,1024,14336]{2,1,0:T(8,128)(2,1)} %hidden.1, bf16[1,1024,4096]{2,1,0:T(8,128)(2,1)} %grad_out.1, bf16[64,14336]{1,0:T(8,128)(2,1)} %proj_in.1, bf16[64,4096]{1,0:T(8,128)(2,1)} %proj_out.1), custom_call_target="tpu_custom_call" | custom-call | flops 2415919104 | bytes 40108032 | tf_op jit(solution)/shard_map/projected_grads/pallas_call | solution.py:258
  27.4 1.7 %covariance.1 = f32[256,2048]{1,0:T(8,128)} custom-call(f32[384,128]{1,0:T(8,128)S(1)} %bitcast.1), custom_call_target="tpu_custom_call" | custom-call | tf_op jit(solution)/shard_map/covariance/pallas_call | solution.py:299

commit v5 on v3

--- a/solution.py
+++ b/solution.py
@@ -10,7 +10,7 @@
 
 MESH = pl.DeviceIdType.MESH
 LANES = 128
-AHEAD = 6
+AHEAD = 18
 
 
 def chunk_of(size, largest=1024):

time: 28.2 us -> 35.9 us (1.27)
  Pallas kernels: 28.1 us -> 35.8 us
    pallas_call x1, Pallas kernels: 26.4 us -> 34.1 us  [shards(): pl.pallas_call(functools.partial(grads_kernel, n_dp, n_tensor, 1.0 / math...]
where the time goes in v5:
time: 35.9 us; the launch traced here: 35.8 us
  Pallas kernels  35.8 us (100%)
    pallas_call x1, Pallas kernels, shards(): pl.pallas_call(functools.partial(grads_kernel, n_dp, n_tensor, 1.0 / math...  34.1 us
    pallas_call x1, Pallas kernels, shards(): pl.pallas_call(functools.partial(covariance_kernel, n_dp, n_tensor, total...  1.72 us

profile of v5, /device:TPU:0, one launch (start us, length us, event | category | flops | bytes accessed | tf_op | source)
XLA Modules:
  0.0 35.8 jit_solution(16412152859478324120)
XLA Ops:
  0.0 34.1 %projected_grads.1 = f32[16,24,128]{2,1,0:T(8,128)S(1)} custom-call(bf16[1,1024,14336]{2,1,0:T(8,128)(2,1)} %hidden.1, bf16[1,1024,4096]{2,1,0:T(8,128)(2,1)} %grad_out.1, bf16[64,14336]{1,0:T(8,128)(2,1)} %proj_in.1, bf16[64,4096]{1,0:T(8,128)(2,1)} %proj_out.1), custom_call_target="tpu_custom_call" | custom-call | flops 2415919104 | bytes 40108032 | tf_op jit(solution)/shard_map/projected_grads/pallas_call | solution.py:248
  34.1 1.7 %covariance.1 = f32[256,2048]{1,0:T(8,128)} custom-call(f32[384,128]{1,0:T(8,128)S(1)} %bitcast.1), custom_call_target="tpu_custom_call" | custom-call | tf_op jit(solution)/shard_map/covariance/pallas_call | solution.py:288

commit v6 on v4

--- a/solution.py
+++ b/solution.py
@@ -10,7 +10,7 @@
 
 MESH = pl.DeviceIdType.MESH
 LANES = 128
-AHEAD = 6
+AHEAD = 3
 
 
 def chunk_of(size, largest=1024):

time: 29.3 us -> 30.8 us (1.051)
  Pallas kernels: 29.2 us -> 30.7 us
    pallas_call x1, Pallas kernels: 27.4 us -> 28.9 us  [shards(): pl.pallas_call(functools.partial(grads_kernel, n_dp, n_tensor, 1.0 / math...]
where the time goes in v6:
time: 30.8 us; the launch traced here: 30.7 us
  Pallas kernels  30.7 us (100%)
    pallas_call x1, Pallas kernels, shards(): pl.pallas_call(functools.partial(grads_kernel, n_dp, n_tensor, 1.0 / math...  28.9 us
    pallas_call x1, Pallas kernels, shards(): pl.pallas_call(functools.partial(covariance_kernel, n_dp, n_tensor, total...  1.72 us

profile of v6, /device:TPU:0, one launch (start us, length us, event | category | flops | bytes accessed | tf_op | source)
XLA Modules:
  0.0 30.7 jit_solution(3323679185089854494)
XLA Ops:
  0.0 28.9 %projected_grads.1 = f32[16,24,128]{2,1,0:T(8,128)S(1)} custom-call(bf16[1,1024,14336]{2,1,0:T(8,128)(2,1)} %hidden.1, bf16[1,1024,4096]{2,1,0:T(8,128)(2,1)} %grad_out.1, bf16[64,14336]{1,0:T(8,128)(2,1)} %proj_in.1, bf16[64,4096]{1,0:T(8,128)(2,1)} %proj_out.1), custom_call_target="tpu_custom_call" | custom-call | flops 2415919104 | bytes 40108032 | tf_op jit(solution)/shard_map/projected_grads/pallas_call | solution.py:258
  29.0 1.7 %covariance.1 = f32[256,2048]{1,0:T(8,128)} custom-call(f32[384,128]{1,0:T(8,128)S(1)} %bitcast.1), custom_call_target="tpu_custom_call" | custom-call | tf_op jit(solution)/shard_map/covariance/pallas_call | solution.py:299

commit v7 on v6

--- a/solution.py
+++ b/solution.py
@@ -10,10 +10,10 @@
 
 MESH = pl.DeviceIdType.MESH
 LANES = 128
-AHEAD = 3
-
-
-def chunk_of(size, largest=1024):
+AHEAD = 12
+
+
+def chunk_of(size, largest=512):
     best = size
     for part in range(LANES, largest + 1, LANES):
         if size % part == 0:
@@ -295,7 +295,7 @@
         name="projected_grads",
     )(*(pltpu.with_memory_space_constraint(x, pltpu.HBM) for x in (hidden, grad_out, proj_in, proj_out)))
     height, wide = total_len // n_dp, total_len // n_tensor
-    block = min(wide, 512)
+    block = min(wide, max(height, 256))
     return pl.pallas_call(
         functools.partial(covariance_kernel, n_dp, n_tensor, total_len),
         out_shape=jax.ShapeDtypeStruct((height, wide), f32),

time: 30.8 us -> 30.2 us (0.981)
  Pallas kernels: 30.7 us -> 30.1 us
    pallas_call x1, Pallas kernels: 28.9 us -> 27.7 us  [shards(): pl.pallas_call(functools.partial(grads_kernel, n_dp, n_tensor, 1.0 / math...]
    pallas_call x1, Pallas kernels: 1.72 us -> 2.38 us  [shards(): pl.pallas_call(functools.partial(covariance_kernel, n_dp, n_tensor, total...]
where the time goes in v7:
time: 30.2 us; the launch traced here: 30.1 us
  Pallas kernels  30.1 us (100%)
    pallas_call x1, Pallas kernels, shards(): pl.pallas_call(functools.partial(grads_kernel, n_dp, n_tensor, 1.0 / math...  27.7 us
    pallas_call x1, Pallas kernels, shards(): pl.pallas_call(functools.partial(covariance_kernel, n_dp, n_tensor, total...  2.38 us

profile of v7, /device:TPU:0, one launch (start us, length us, event | category | flops | bytes accessed | tf_op | source)
XLA Modules:
  0.0 30.1 jit_solution(8298259607717045487)
XLA Ops:
  0.0 27.7 %projected_grads.1 = f32[16,24,128]{2,1,0:T(8,128)S(1)} custom-call(bf16[1,1024,14336]{2,1,0:T(8,128)(2,1)} %hidden.1, bf16[1,1024,4096]{2,1,0:T(8,128)(2,1)} %grad_out.1, bf16[64,14336]{1,0:T(8,128)(2,1)} %proj_in.1, bf16[64,4096]{1,0:T(8,128)(2,1)} %proj_out.1), custom_call_target="tpu_custom_call" | custom-call | flops 2415919104 | bytes 40108032 | tf_op jit(solution)/shard_map/projected_grads/pallas_call | solution.py:258
  27.7 2.4 %covariance.1 = f32[256,2048]{1,0:T(8,128)} custom-call(f32[384,128]{1,0:T(8,128)S(1)} %bitcast.1), custom_call_target="tpu_custom_call" | custom-call | tf_op jit(solution)/shard_map/covariance/pallas_call | solution.py:299

commit v8 on v4

--- a/solution.py
+++ b/solution.py
@@ -177,22 +177,26 @@
         message[d, own_rows:own_rows + row_rows] = grads[d * row_rows:(d + 1) * row_rows]
         message[d, own_rows + row_rows:used] = square
 
-    def message_copy(i):
-        to = lax.rem(dp + i, n_dp)
+    def message_copy(k):
+        to = k + (k >= dp).astype(jnp.int32)
+        slot = lax.rem(to - dp + n_dp, n_dp)
         return pltpu.make_async_remote_copy(
             src_ref=message.at[to, pl.ds(0, used)],
-            dst_ref=gathered.at[i, pl.ds(0, used)],
-            send_sem=message_send.at[i],
-            recv_sem=message_recv.at[i],
+            dst_ref=gathered.at[slot, pl.ds(0, used)],
+            send_sem=message_send.at[k],
+            recv_sem=message_recv.at[slot],
             device_id=(to, ts),
             device_id_type=MESH,
         )
 
-    for i in sorted(range(1, n_dp), key=lambda i: -min(i, n_dp - i)):
-        message_copy(i).start()
+    for k in range(n_dp - 1):
+        message_copy(k).start()
     gathered[0] = message[dp]
     for i in range(1, n_dp):
-        message_copy(i).wait()
+        arrived = gathered.at[i, pl.ds(0, used)]
+        pltpu.make_async_copy(arrived, arrived, message_recv.at[i]).wait()
+    for k in range(n_dp - 1):
+        message_copy(k).wait_send()
 
 
 def covariance_kernel(n_dp, n_tensor, total_len, gathered, out, block_sem, result):
@@ -225,14 +229,15 @@
         right_high, right_low = high_low(b * here, here)
         right = jnp.concatenate([right_high, right_high, right_low], axis=0).astype(jnp.bfloat16)
         result[b] = jnp.dot(left, right, preferred_element_type=jnp.float32)
-        for k in range(block // height):
-            @pl.when(diagonal == b * block + k * height)
-            def _():
-                for r in range(row_rows):
-                    place = (pl.ds(r * LANES, LANES), pl.ds(k * height + r * LANES, LANES))
-                    ids = lax.broadcasted_iota(jnp.int32, (LANES, LANES), 0)
-                    same = ids == lax.broadcasted_iota(jnp.int32, (LANES, LANES), 1)
-                    result[(b, *place)] += jnp.where(same, damping, jnp.float32(0.0))
+        @pl.when(jnp.logical_and(diagonal >= b * block, diagonal < (b + 1) * block))
+        def _():
+            for r in range(row_rows):
+                first = pl.multiple_of(diagonal - b * block + r * LANES, LANES)
+                place = (pl.ds(r * LANES, LANES), pl.ds(first, LANES))
+                ids = lax.broadcasted_iota(jnp.int32, (LANES, LANES), 0)
+                same = ids == lax.broadcasted_iota(jnp.int32, (LANES, LANES), 1)
+                result[(b, *place)] += jnp.where(same, damping, jnp.float32(0.0))
+
         block_copy(b).start()
     for b in range(blocks):
         block_copy(b).wait()
@@ -295,7 +300,7 @@
         name="projected_grads",
     )(*(pltpu.with_memory_space_constraint(x, pltpu.HBM) for x in (hidden, grad_out, proj_in, proj_out)))
     height, wide = total_len // n_dp, total_len // n_tensor
-    block = min(wide, 512)
+    block = min(wide, 1024)
     return pl.pallas_call(
         functools.partial(covariance_kernel, n_dp, n_tensor, total_len),
         out_shape=jax.ShapeDtypeStruct((height, wide), f32),

time: 29.3 us -> 28.1 us (0.959)
  Pallas kernels: 29.2 us -> 28 us
    pallas_call x1, Pallas kernels: 27.4 us -> 26.3 us  [shards(): pl.pallas_call(functools.partial(grads_kernel, n_dp, n_tensor, 1.0 / math...]
where the time goes in v8:
time: 28.1 us; the launch traced here: 28 us
  Pallas kernels  28 us (100%)
    pallas_call x1, Pallas kernels, shards(): pl.pallas_call(functools.partial(grads_kernel, n_dp, n_tensor, 1.0 / math...  26.3 us
    pallas_call x1, Pallas kernels, shards(): pl.pallas_call(functools.partial(covariance_kernel, n_dp, n_tensor, total...  1.71 us

profile of v8, /device:TPU:0, one launch (start us, length us, event | category | flops | bytes accessed | tf_op | source)
XLA Modules:
  0.0 28.0 jit_solution(11009657156938951942)
XLA Ops:
  0.0 26.3 %projected_grads.1 = f32[16,24,128]{2,1,0:T(8,128)S(1)} custom-call(bf16[1,1024,14336]{2,1,0:T(8,128)(2,1)} %hidden.1, bf16[1,1024,4096]{2,1,0:T(8,128)(2,1)} %grad_out.1, bf16[64,14336]{1,0:T(8,128)(2,1)} %proj_in.1, bf16[64,4096]{1,0:T(8,128)(2,1)} %proj_out.1), custom_call_target="tpu_custom_call" | custom-call | flops 2415919104 | bytes 40108032 | tf_op jit(solution)/shard_map/projected_grads/pallas_call | solution.py:263
  26.3 1.7 %covariance.1 = f32[256,2048]{1,0:T(8,128)} custom-call(f32[384,128]{1,0:T(8,128)S(1)} %bitcast.1), custom_call_target="tpu_custom_call" | custom-call | tf_op jit(solution)/shard_map/covariance/pallas_call | solution.py:304

commit v9 on v8

--- a/solution.py
+++ b/solution.py
@@ -11,6 +11,7 @@
 MESH = pl.DeviceIdType.MESH
 LANES = 128
 AHEAD = 6
+FIRST = 2
 
 
 def chunk_of(size, largest=1024):
@@ -80,14 +81,16 @@
 
     copies = [(wo_copy, g_copy, c) for c in range(g_chunks)] + [(wi_copy, h_copy, c) for c in range(h_chunks)]
 
-    def begin(k):
-        if k < len(copies):
-            weight, data, c = copies[k]
+    begun = [0]
+
+    def begin(arrived):
+        until = min(FIRST + 2 * arrived, arrived + AHEAD, len(copies))
+        for weight, data, c in copies[begun[0]:until]:
             weight(c).start()
             data(c).start()
-
-    for k in range(AHEAD):
-        begin(k)
+        begun[0] = max(begun[0], until)
+
+    begin(0)
 
     barrier = pltpu.get_barrier_semaphore()
     n_all = n_dp * n_tensor
@@ -105,7 +108,7 @@
         for c in group:
             weight_copy(c).wait()
             data_copy(c).wait()
-            begin(before + c + AHEAD)
+            begin(before + c + 1)
         term = contract_last(weights[group[0]], data[group[0]])
         for c in group[1:]:
             term = term + contract_last(weights[c], data[c])
@@ -114,7 +117,7 @@
         else:
             panel[...] += term
 
-    for group in groups_of(g_chunks, 1, 0):
+    for group in groups_of(g_chunks, g_chunks, 0):
         project(group, wo_buf, g_buf, wo_copy, g_copy, 0, out_panel)
 
     pl.semaphore_wait(barrier, n_all - 1)
@@ -132,7 +135,7 @@
     for i in range(1, n_tensor):
         panel_copy(i).start()
 
-    in_groups = groups_of(h_chunks, 0, 2)
+    in_groups = groups_of(h_chunks, h_chunks, 0)
     for group in in_groups[:-1]:
         project(group, wi_buf, h_buf, wi_copy, h_copy, g_chunks, in_panel)
     for i in range(1, n_tensor):

time: 28.1 us -> 28.5 us (1.014)
  Pallas kernels: 28 us -> 28.3 us
    pallas_call x1, Pallas kernels: 26.3 us -> 26.6 us  [shards(): pl.pallas_call(functools.partial(grads_kernel, n_dp, n_tensor, 1.0 / math...]
where the time goes in v9:
time: 28.5 us; the launch traced here: 28.3 us
  Pallas kernels  28.3 us (99%)
    pallas_call x1, Pallas kernels, shards(): pl.pallas_call(functools.partial(grads_kernel, n_dp, n_tensor, 1.0 / math...  26.6 us
    pallas_call x1, Pallas kernels, shards(): pl.pallas_call(functools.partial(covariance_kernel, n_dp, n_tensor, total...  1.7 us

profile of v9, /device:TPU:0, one launch (start us, length us, event | category | flops | bytes accessed | tf_op | source)
XLA Modules:
  0.0 28.3 jit_solution(14748021182563860664)
XLA Ops:
  0.0 26.6 %projected_grads.1 = f32[16,24,128]{2,1,0:T(8,128)S(1)} custom-call(bf16[1,1024,14336]{2,1,0:T(8,128)(2,1)} %hidden.1, bf16[1,1024,4096]{2,1,0:T(8,128)(2,1)} %grad_out.1, bf16[64,14336]{1,0:T(8,128)(2,1)} %proj_in.1, bf16[64,4096]{1,0:T(8,128)(2,1)} %proj_out.1), custom_call_target="tpu_custom_call" | custom-call | flops 2415919104 | bytes 40108032 | tf_op jit(solution)/shard_map/projected_grads/pallas_call | solution.py:266
  26.6 1.7 %covariance.1 = f32[256,2048]{1,0:T(8,128)} custom-call(f32[384,128]{1,0:T(8,128)S(1)} %bitcast.1), custom_call_target="tpu_custom_call" | custom-call | tf_op jit(solution)/shard_map/covariance/pallas_call | solution.py:307

commit v10 on v9

--- a/solution.py
+++ b/solution.py
@@ -10,8 +10,8 @@
 
 MESH = pl.DeviceIdType.MESH
 LANES = 128
-AHEAD = 6
-FIRST = 2
+AHEAD = 8
+FIRST = 4
 
 
 def chunk_of(size, largest=1024):

time: 28.5 us -> 27.6 us (0.968)
  Pallas kernels: 28.3 us -> 27.4 us
    pallas_call x1, Pallas kernels: 26.6 us -> 25.7 us  [shards(): pl.pallas_call(functools.partial(grads_kernel, n_dp, n_tensor, 1.0 / math...]
where the time goes in v10:
time: 27.6 us; the launch traced here: 27.4 us
  Pallas kernels  27.4 us (99%)
    pallas_call x1, Pallas kernels, shards(): pl.pallas_call(functools.partial(grads_kernel, n_dp, n_tensor, 1.0 / math...  25.7 us
    pallas_call x1, Pallas kernels, shards(): pl.pallas_call(functools.partial(covariance_kernel, n_dp, n_tensor, total...  1.7 us

profile of v10, /device:TPU:0, one launch (start us, length us, event | category | flops | bytes accessed | tf_op | source)
XLA Modules:
  0.0 27.4 jit_solution(1302522931015994624)
XLA Ops:
  0.0 25.7 %projected_grads.1 = f32[16,24,128]{2,1,0:T(8,128)S(1)} custom-call(bf16[1,1024,14336]{2,1,0:T(8,128)(2,1)} %hidden.1, bf16[1,1024,4096]{2,1,0:T(8,128)(2,1)} %grad_out.1, bf16[64,14336]{1,0:T(8,128)(2,1)} %proj_in.1, bf16[64,4096]{1,0:T(8,128)(2,1)} %proj_out.1), custom_call_target="tpu_custom_call" | custom-call | flops 2415919104 | bytes 40108032 | tf_op jit(solution)/shard_map/projected_grads/pallas_call | solution.py:266
  25.7 1.7 %covariance.1 = f32[256,2048]{1,0:T(8,128)} custom-call(f32[384,128]{1,0:T(8,128)S(1)} %bitcast.1), custom_call_target="tpu_custom_call" | custom-call | tf_op jit(solution)/shard_map/covariance/pallas_call | solution.py:307
